TPU v7x, 256 devices: a whole 4x4x8 slice. The times are simulated.
256 devices in a mesh: cam: 16 (over y, x), blk: 16 (over z, core).
Axes of the slice: x: 4, y: 4, z: 8, core: 2. Of those that a mesh axis runs over, the one named last changes fastest.
Arguments:
- cam_index: int32 [16, 16, 2, 16, 128], P('cam', 'blk'), may hold values from 0 to 64, as said below
- point_index: int32 [16, 16, 2, 16, 128], P('cam', 'blk'), may hold values from 0 to 31
- jac_cam: float32 [16, 16, 2, 12, 16, 128], P('cam', 'blk'), may hold values from -12 to 12
- jac_point: float32 [16, 16, 2, 6, 16, 128], P('cam', 'blk'), may hold values from -0.9 to 0.9
- point_damping: float32 [16, 16, 32], P('cam', 'blk'), may hold values from 0.1 to 1
Outputs:
- schur_band: float32 [98304, 6144], P(('cam', 'blk'))
Inputs may be any that keep to these rules, and one draw needn't show every extreme that they name: `cam_index`: 64 marks an empty slot; every slot with p = 1 in the bands of the last segment is empty.
All inputs are finite; a program needn't handle non-finite values.
Results may differ from a plain program's by a relative error of at most 0.0034.
Values may be sent and summed in bfloat16 or wider, within the bound.
No kernel may reach another device: no remote copies, remote signals or barrier semaphores. Data moves between devices by JAX's collectives and lax.ppermute only.
A program may use at most 256 MiB of HBM per device.

v0:
```python
import jax
import jax.numpy as jnp
from jax import lax
from jax.sharding import PartitionSpec as P

NCAM = 64


PAIRS = ((0, 0), (0, 1), (0, 2), (1, 1), (1, 2), (2, 2))
DIAG_MASK = (1.0, 0.0, 0.0, 1.0, 0.0, 1.0)


def shifted(shard, axis, by):
    length = lax.axis_size(axis)
    pairs = [(i, i + by) for i in range(length) if 0 <= i + by < length]
    return lax.ppermute(shard, axis, pairs)


def products(tracks):
    return jnp.stack(
        [
            tracks[band_position] * tracks[j] + tracks[3 + band_position] * tracks[3 + j]
            for band_position, j in PAIRS
        ]
    )


def factor(sym):
    root_first = jnp.sqrt(sym[0])
    low_second = sym[1] / root_first
    low_third = sym[2] / root_first
    root_second = jnp.sqrt(sym[3] - low_second * low_second)
    low_mixed = (sym[4] - low_third * low_second) / root_second
    root_third = jnp.sqrt(sym[5] - low_third * low_third - low_mixed * low_mixed)
    inv_first = 1.0 / root_first
    inv_second = 1.0 / root_second
    inv_third = 1.0 / root_third
    inv_lower = -inv_second * low_second * inv_first
    inv_mixed = -inv_third * low_mixed * inv_second
    inv_corner = -(inv_mixed * low_second + inv_third * low_third) * inv_first
    return jnp.stack([inv_first, inv_lower, inv_second, inv_corner, inv_mixed, inv_third])


def eliminate_points(tracks, looked):
    rows = []
    for row in range(2):
        first = tracks[3 * row]
        second = tracks[3 * row + 1]
        third = tracks[3 * row + 2]
        rows.append(first * looked[0])
        rows.append(first * looked[1] + second * looked[2])
        rows.append(first * looked[3] + second * looked[4] + third * looked[5])
    return jnp.stack(rows)


def contribution_list(camera_row_block, eliminated_tile):
    return jnp.stack(
        [
            camera_row_block[offset_step] * eliminated_tile[band_position]
            + camera_row_block[6 + offset_step] * eliminated_tile[3 + band_position]
            for offset_step in range(6)
            for band_position in range(3)
        ]
    )


def build_panel(values, bins, width):
    summed = jax.ops.segment_sum(values.T, bins, num_segments=NCAM * width)
    return (
        summed.reshape(NCAM, width, 6, 3)
        .transpose(0, 2, 3, 1)
        .reshape(NCAM * 6, 3 * width)
        .astype(jnp.bfloat16)
    )


def outer(left, right):
    return lax.dot_general(
        left, right, (((1,), (1,)), ((), ())), preferred_element_type=jnp.float32
    )


def body(cam_index, point_index, jac_cam, jac_point, point_damping):
    cameras = cam_index.reshape(cam_index.shape[2:])
    places = point_index.reshape(point_index.shape[2:])
    nblk = cameras.shape[1]
    damping = point_damping.reshape(-1)
    npts = damping.shape[0]
    live = (cameras < NCAM).astype(jnp.float32)
    camera_row_block = jnp.moveaxis(jac_cam.reshape(jac_cam.shape[2:]), 1, 0) * live
    tracks = jnp.moveaxis(jac_point.reshape(jac_point.shape[2:]), 1, 0) * live
    forward = shifted((tracks[:, 1], places[1]), "cam", 1)
    outgoing = jnp.stack([tracks[:, 0], forward[0]], axis=1)
    spots = jnp.stack([places[0], forward[1]])[None]
    received_tracks, received_spots = (
        lax.all_to_all(outgoing, "blk", split_axis=2, concat_axis=2, tiled=True),
        lax.all_to_all(spots, "blk", split_axis=2, concat_axis=2, tiled=True),
    )
    onehot = (received_spots[0][..., None] == jnp.arange(npts, dtype=jnp.int32)).astype(jnp.float32)
    sums = jnp.einsum(
        "qaso,asop->qp", products(received_tracks), onehot, precision=lax.Precision.HIGHEST
    )
    sums = sums + damping[None, :] * jnp.array(DIAG_MASK, jnp.float32)[:, None]
    lookup_table = factor(sums)
    eliminated_remote = eliminate_points(
        received_tracks, jnp.take(lookup_table, received_spots[0], axis=1)
    )
    eliminated_previous = lax.all_to_all(
        eliminated_remote, "blk", split_axis=2, concat_axis=2, tiled=True
    )
    eliminated_following = shifted(eliminated_previous[:, 1], "cam", -1)
    eliminated_tile = jnp.stack([eliminated_previous[:, 0], eliminated_following], axis=1)
    schur_contribution = contribution_list(camera_row_block, eliminated_tile)
    width = 2 * nblk * npts
    part_ids = lax.broadcasted_iota(jnp.int32, places.shape, 0)
    block_ids = lax.broadcasted_iota(jnp.int32, places.shape, 1)
    bins = ((cameras * 2 + part_ids) * nblk + block_ids) * npts + places
    flat_bins = jnp.minimum(bins, NCAM * width - 1).reshape(-1)
    values = schur_contribution.reshape(18, -1)
    panel = build_panel(values, flat_bins, width)
    return outer(panel, lax.all_gather(panel, "blk", axis=0, tiled=True))


def solution(mesh):
    return jax.shard_map(
        body,
        mesh=mesh,
        in_specs=(
            P("cam", "blk", None, None, None),
            P("cam", "blk", None, None, None),
            P("cam", "blk", None, None, None, None),
            P("cam", "blk", None, None, None, None),
            P("cam", "blk", None),
        ),
        out_specs=P(("cam", "blk"), None),
        check_vma=False,
    )
```

profile of v0, /device:TPU:1, one launch (start us, length us, event | category | flops | bytes accessed | tf_op | source)
XLA Modules:
  0.0 362.8 jit_solution(10257931083743953459)
XLA Ops:
  7.3 3.9 %collective-permute-start.1 = (s32[16,128]{1,0:T(8,128)S(1)}, s32[16,128]{1,0:T(8,128)S(1)}, u32[]{:S(2)}, u32[]{:S(2)}) collective-permute-start(s32[16,128]{1,0:T(8,128)S(1)} %get-tuple-element.66), channel_id=1, source_target_pairs={{0,16},{16,32},{32,48},{48,64},{64,80},{80,96},{96,112},{112,128},... | collective-permute-start | bytes 24584 | tf_op jit(solution)/shard_map/ppermute | solution.py:16
  11.2 0.7 convert_bitcast_fusion
  11.9 0.9 fusion.5
  12.8 3.1 collective-permute-start
  16.6 9.7 %all-to-all-start.1 = ((s32[1,2,16,128]{3,1,0,2:T(2,128)}), s32[1,2,16,128]{3,1,0,2:T(2,128)S(1)}, u32[]{:S(2)}, u32[]{:S(2)}) async-start(s32[1,2,16,128]{3,1,0,2:T(2,128)} %add_bitcast_fusion), calls=%async_computation.1 | async-start | bytes 32768 | tf_op jit(solution)/shard_map/all_to_all | solution.py:97
  26.3 0.7 broadcast_multiply_fusion
  27.0 6.6 %all-to-all-done.1 = s32[1,2,16,128]{3,1,0,2:T(2,128)S(1)} async-done(((s32[1,2,16,128]{3,1,0,2:T(2,128)}), s32[1,2,16,128]{3,1,0,2:T(2,128)S(1)}, u32[]{:S(2)}, u32[]{:S(2)}) %all-to-all-start.1) | async-done | bytes 16416 | tf_op jit(solution)/shard_map/all_to_all | solution.py:97
  33.7 0.7 copy.91
  34.5 3.7 %all-to-all-start = ((f32[6,2,16,128]{3,1,0,2:T(2,128)}), f32[6,2,16,128]{3,1,0,2:T(2,128)S(1)}, u32[]{:S(2)}, u32[]{:S(2)}) async-start(f32[6,2,16,128]{3,1,0,2:T(2,128)} %copy.91), calls=%async_computation | async-start | bytes 196608 | tf_op jit(solution)/shard_map/all_to_all | solution.py:96
  38.2 8.5 %all-to-all-done = f32[6,2,16,128]{3,1,0,2:T(2,128)S(1)} async-done(((f32[6,2,16,128]{3,1,0,2:T(2,128)}), f32[6,2,16,128]{3,1,0,2:T(2,128)S(1)}, u32[]{:S(2)}, u32[]{:S(2)}) %all-to-all-start) | async-done | bytes 98336 | tf_op jit(solution)/shard_map/all_to_all | solution.py:96
  47.0 1.0 fusion.2
  48.2 10.8 %gather_fusion = f32[4096,6]{1,0:T(8,128)S(1)} fusion(f32[6,32]{0,1:T(8,128)S(1)} %copy.101, s32[4096]{0:T(1024)S(1)} %broadcast_clamp_fusion), kind=kCustom, calls=%fused_computation | custom fusion | bytes 212992 | tf_op jit(solution)/shard_map/jit(_take)/gather | solution.py:106
  59.9 0.7 copy.104
  60.7 3.4 all-to-all-start.2
  64.2 8.2 %all-to-all-done.2 = f32[6,2,16,128]{3,1,0,2:T(2,128)S(1)} async-done(((f32[6,2,16,128]{3,1,0,2:T(2,128)}), f32[6,2,16,128]{3,1,0,2:T(2,128)S(1)}, u32[]{:S(2)}, u32[]{:S(2)}) %all-to-all-start.2) | async-done | bytes 98336 | tf_op jit(solution)/shard_map/all_to_all | solution.py:108
  72.5 1.3 collective-permute-start.2
  73.9 4.0 %collective-permute-done.2 = f32[6,16,128]{2,1,0:T(8,128)S(1)} collective-permute-done((f32[6,16,128]{2,1,0:T(8,128)S(1)}, f32[6,16,128]{2,1,0:T(8,128)S(1)}, u32[]{:S(2)}, u32[]{:S(2)}) %collective-permute-start.2) | collective-permute-done | bytes 49184 | tf_op jit(solution)/shard_map/ppermute | solution.py:16
  79.0 35.5 %scatter_custom_fusion = f32[65536,18]{1,0:T(8,128)} fusion(s32[4096]{0:T(1024)S(1)} %bitcast.116, f32[4096,18]{1,0:T(8,128)S(1)} %copy.107, f32[]{:T(128)} %constant.11.clone.1), kind=kCustom, calls=%fused_computation.2 | custom fusion | flops 73728 | bytes 4718596 | tf_op jit(solution)/shard_map/scatter-add | solution.py:68
  114.6 18.8 %copy.108 = bf16[65536,18]{0,1:T(8,128)(2,1)S(1)} copy(f32[65536,18]{1,0:T(8,128)} %scatter_custom_fusion) | data formatting | bytes 7077888 | tf_op jit(solution)/shard_map/scatter-add | solution.py:68
  133.3 1.7 copy.121
  135.3 2.0 copy.109
  137.3 2.5 copy.122
  139.9 193.4 %all-gather.2.cloned.1.call-done = bf16[6144,3072]{1,0:T(8,128)(2,1)} async-done(((bf16[384,3072]{1,0:T(8,128)(2,1)}), bf16[6144,3072]{1,0:T(8,128)(2,1)}) %all-gather.2.cloned.1.call-update) | async-done | bytes 37748752 | tf_op jit(solution)/shard_map/all_gather | solution.py:121
  333.2 22.8 %fusion.20 = f32[384,6144]{1,0:T(8,128)} fusion(bf16[384,3072]{1,0:T(8,128)(2,1)} %bitcast.84, bf16[6144,3072]{1,0:T(8,128)(2,1)} %all-gather.2.cloned.1.call-done), kind=kOutput, calls=%fused_computation.90 | convolution fusion | flops 14495514624 | bytes 49545216 | tf_op jit(solution)/shard_map/dot_general | solution.py:78
  (42 shorter events, 4.4 us)
Async XLA Ops:
  7.3 8.7 %collective-permute-start.1 = (s32[16,128]{1,0:T(8,128)S(1)}, s32[16,128]{1,0:T(8,128)S(1)}, u32[]{:S(2)}, u32[]{:S(2)}) collective-permute-start(s32[16,128]{1,0:T(8,128)S(1)} %get-tuple-element.66), channel_id=1, source_target_pairs={{0,16},{16,32},{32,48},{48,64},{64,80},{80,96},{96,112},{112,128},... | collective-permute-start | bytes 24584 | tf_op jit(solution)/shard_map/ppermute | solution.py:16
  12.8 51.3 %copy-start.1 = (s32[1,1,2,16,128]{4,3,2,1,0:T(8,128)S(1)}, s32[1,1,2,16,128]{4,3,2,1,0:T(8,128)}, u32[]{:S(2)}) copy-start(s32[1,1,2,16,128]{4,3,2,1,0:T(8,128)} %param.7) | copy-start | bytes 49156
  12.8 20.9 %collective-permute-start = (f32[6,16,128]{2,1,0:T(8,128)S(1)}, f32[6,16,128]{2,1,0:T(8,128)S(1)}, u32[]{:S(2)}, u32[]{:S(2)}) collective-permute-start(f32[6,16,128]{2,1,0:T(8,128)S(1)} %get-tuple-element.58), channel_id=1, source_target_pairs={{0,16},{16,32},{32,48},{48,64},{64,80},{80,96},{96,112},{112,128},... | collective-permute-start | bytes 147464 | tf_op jit(solution)/shard_map/ppermute | solution.py:16
  16.6 17.0 %all-to-all-start.1 = ((s32[1,2,16,128]{3,1,0,2:T(2,128)}), s32[1,2,16,128]{3,1,0,2:T(2,128)S(1)}, u32[]{:S(2)}, u32[]{:S(2)}) async-start(s32[1,2,16,128]{3,1,0,2:T(2,128)} %add_bitcast_fusion), calls=%async_computation.1 | async-start | bytes 32768 | tf_op jit(solution)/shard_map/all_to_all | solution.py:97
  33.7 40.1 %copy-start = (f32[1,1,2,12,16,128]{5,4,3,2,1,0:T(8,128)S(1)}, f32[1,1,2,12,16,128]{5,4,3,2,1,0:T(8,128)}, u32[]{:S(2)}) copy-start(f32[1,1,2,12,16,128]{5,4,3,2,1,0:T(8,128)} %param.8) | copy-start | bytes 589828
  34.5 12.2 %all-to-all-start = ((f32[6,2,16,128]{3,1,0,2:T(2,128)}), f32[6,2,16,128]{3,1,0,2:T(2,128)S(1)}, u32[]{:S(2)}, u32[]{:S(2)}) async-start(f32[6,2,16,128]{3,1,0,2:T(2,128)} %copy.91), calls=%async_computation | async-start | bytes 196608 | tf_op jit(solution)/shard_map/all_to_all | solution.py:96
  60.7 11.8 %all-to-all-start.2 = ((f32[6,2,16,128]{3,1,0,2:T(2,128)}), f32[6,2,16,128]{3,1,0,2:T(2,128)S(1)}, u32[]{:S(2)}, u32[]{:S(2)}) async-start(f32[6,2,16,128]{3,1,0,2:T(2,128)} %copy.104), calls=%async_computation.2 | async-start | bytes 196608 | tf_op jit(solution)/shard_map/all_to_all | solution.py:108
  64.1 269.2 %all-gather.2.cloned.1.call-start = ((), (), s32[]{:S(2)}) async-start(), calls=%async_computation.3 | async-start | bytes 40108032 | tf_op jit(solution)/shard_map/all_gather | solution.py:121
  72.5 5.3 %collective-permute-start.2 = (f32[6,16,128]{2,1,0:T(8,128)S(1)}, f32[6,16,128]{2,1,0:T(8,128)S(1)}, u32[]{:S(2)}, u32[]{:S(2)}) collective-permute-start(f32[6,16,128]{2,1,0:T(8,128)S(1)} %bitcast.112), channel_id=1, source_target_pairs={{16,0},{32,16},{48,32},{64,48},{80,64},{96,80},{112,96},{128,112},... | collective-permute-start | bytes 147464 | tf_op jit(solution)/shard_map/ppermute | solution.py:16
Sparse Core Ops, SparseCore 0:
  140.0 193.1 all-gather.1
where the time goes:
time: 364 us; the launch traced here: 363 us
  waiting for transfers between devices  221 us (61%)
  local copies, waits for them, and re-layouts  40.5 us (11%)
  other arithmetic  39 us (11%)
  starting transfers between devices  25.2 us (7%)
  matrix products  23.8 us (7%)
  between operations  13.7 us (4%)
    all_gather x1, waiting for transfers between devices, body(): return outer(panel, lax.all_gather(panel, 'blk', axis=0, tiled=True))  193 us
    scatter-add x1, other arithmetic, build_panel(): summed = jax.ops.segment_sum(values.T, bins, num_segments=NCAM * width)  35.5 us
    dot_general x1, matrix products, outer(): lax.dot_general(left, right, (((1,), (1,)), ((), ())), preferred_element_...  22.8 us
    scatter-add x1, local copies, waits for them, and re-layouts, build_panel(): summed = jax.ops.segment_sum(values.T, bins, num_segments=NCAM * width)  18.8 us
    gather x2, local copies, waits for them, and re-layouts, body(): jnp.take(lookup_table, received_spots[0], axis=1)  11.4 us
    all_to_all x1, starting transfers between devices, body(): lax.all_to_all(spots, 'blk', split_axis=2, concat_axis=2, tiled=True)  9.71 us
    all_to_all x1, waiting for transfers between devices, body(): lax.all_to_all(outgoing, 'blk', split_axis=2, concat_axis=2, tiled=True)  8.51 us
    ppermute x3, starting transfers between devices, shifted(): return lax.ppermute(shard, axis, pairs)  8.35 us
  transfers between devices with their start and end apart: 7, of which 5 were waited for; matrix products, arithmetic and copies ran while one was open for 1% of the time, Pallas kernels for 0%

commit v1 on v0

v1 whole, which is shorter than its diff:
```python
import functools

import jax
import jax.numpy as jnp
from jax import lax
from jax.experimental import pallas as pl
from jax.experimental.pallas import tpu as pltpu
from jax.sharding import PartitionSpec as P

F32 = jnp.float32
BF16 = jnp.bfloat16
NT = (((1,), (1,)), ((), ()))
NCAM = 64
NBLK = 16
PTS = 32
Q = 2 * NBLK
ROWS = NCAM * 6
DEPTH = 3 * PTS * Q
VALS = 26
PAIRS = ((0, 0), (0, 1), (0, 2), (1, 1), (1, 2), (2, 2))


def vmem():
    return pl.BlockSpec(memory_space=pltpu.VMEM)


def smem():
    return pl.BlockSpec(memory_space=pltpu.SMEM)


def params():
    return pltpu.CompilerParams(vmem_limit_bytes=56 * 2**20)


def split(x):
    hi = x.astype(BF16).astype(F32)
    return hi, x - hi


def prepare(ids, cam, pt, jac_cam, jac_point, damping, payload, mine, other, prods):
    core = lax.rem(ids[0], 2)
    lane = lax.broadcasted_iota(jnp.int32, (8, 128), 1)
    entry = lax.broadcasted_iota(jnp.int32, (8, 128), 0)
    diag = (entry == 0) | (entry == 3) | (entry == 5)
    damp = jnp.broadcast_to(jnp.concatenate([damping[...]] * 4, axis=1), (8, 128))
    damp = jnp.where(diag & (lane // PTS == lax.rem(ids[0], 4)), damp, 0.0)
    rows128 = lax.broadcasted_iota(jnp.int32, (128, 128), 0)
    totals = []
    for p in range(2):
        span = pl.ds(p * NBLK, NBLK)
        cams = cam[span]
        live = (cams < NCAM).astype(F32)
        payload[24, span] = cams.astype(F32).astype(BF16)
        payload[25, span] = pt[span].astype(F32).astype(BF16)
        for v in range(12):
            payload[v, span] = jac_cam[p, v].astype(BF16)
        tracks = [jac_point[p, v] * live for v in range(6)]
        for v in range(6):
            hi, lo = split(tracks[v])
            payload[12 + v, span] = hi.astype(BF16)
            payload[18 + v, span] = lo.astype(BF16)
        for e, (i, j) in enumerate(PAIRS):
            prods[span, e] = tracks[i] * tracks[j] + tracks[3 + i] * tracks[3 + j]
        prods[span, 6] = jnp.zeros((NBLK, 128), F32)
        prods[span, 7] = jnp.zeros((NBLK, 128), F32)
        for g in range(4):
            left = []
            right = []
            for t in range(4):
                q = p * NBLK + 4 * g + t
                hi, rest = split(prods[q])
                mid, low = split(rest)
                left.append(jnp.concatenate([hi, mid, low, jnp.zeros((8, 128), F32)], axis=0).astype(BF16))
                spot = jnp.broadcast_to(pt[pl.ds(q, 1)], (128, 128)) + PTS * t
                right.append(jnp.where(spot == rows128, 1.0, 0.0).astype(BF16))
            got = lax.dot_general(
                jnp.concatenate(left, axis=1), jnp.concatenate(right, axis=1), NT, preferred_element_type=F32
            )
            total = got[0:8] + got[8:16] + got[16:24]
            if p == 0:
                total = total + jnp.where(ids[0] // 4 == g, damp, 0.0)
            totals.append(total)
    for g in range(4):
        mine[g] = jnp.where(core == 0, totals[g], totals[4 + g])
        other[g] = jnp.where(core == 0, totals[4 + g], totals[g])


def factor(parts, inverse):
    total = parts[0]
    for n in range(1, 16):
        total = total + parts[n]
    sym = [total[:, e, :] for e in range(6)]
    root_first = jnp.sqrt(sym[0])
    low_second = sym[1] / root_first
    low_third = sym[2] / root_first
    root_second = jnp.sqrt(sym[3] - low_second * low_second)
    low_mixed = (sym[4] - low_third * low_second) / root_second
    root_third = jnp.sqrt(sym[5] - low_third * low_third - low_mixed * low_mixed)
    inv_first = 1.0 / root_first
    inv_second = 1.0 / root_second
    inv_third = 1.0 / root_third
    inv_lower = -inv_second * low_second * inv_first
    inv_mixed = -inv_third * low_mixed * inv_second
    inv_corner = -(inv_mixed * low_second + inv_third * low_third) * inv_first
    for e, x in enumerate((inv_first, inv_lower, inv_second, inv_corner, inv_mixed, inv_third)):
        inverse[e] = x


def eliminate(tracks, spots, table, rows_out):
    offset = lax.rem(lax.broadcasted_iota(jnp.int32, (Q, 128), 0), 4) * PTS
    where = spots + offset
    looked = [jnp.take_along_axis(table[e], where, axis=1) for e in range(6)]
    for r in range(2):
        first, second, third = tracks[3 * r : 3 * r + 3]
        rows_out[3 * r] = first * looked[0]
        rows_out[3 * r + 1] = first * looked[1] + second * looked[2]
        rows_out[3 * r + 2] = first * looked[3] + second * looked[4] + third * looked[5]


def hot(spot, count):
    rows = lax.broadcasted_iota(jnp.int32, (count, 128), 0).astype(F32)
    return jnp.where(jnp.broadcast_to(spot, (count, 128)) == rows, 1.0, 0.0).astype(BF16)


def spread(row, mask):
    value = jnp.broadcast_to(row, (16, 128)).astype(BF16)
    return jnp.concatenate([value] * (mask.shape[0] // 16), axis=0) * mask


def relayout(tile, store):
    low = lax.broadcasted_iota(jnp.int32, (PTS, 128), 1) < NCAM
    for m in range(3):
        even = tile[64 * m : 64 * m + 32]
        odd = tile[64 * m + 32 : 64 * m + 64]
        even_rolled = pltpu.roll(even[:, :128], 64, axis=1)
        odd_rolled = pltpu.roll(odd[:, :128], 64, axis=1)
        store(0, m, jnp.where(low, even[:, :128], odd_rolled))
        store(1, m, jnp.where(low, even_rolled, odd[:, :128]))
        store(2, m, jnp.where(low, even[:, 128:], odd[:, 128:]))


def own_panel(ids, cam, pt, jac_cam, jac_point, inv_mine, inv_other, panel, table, rows_e, rows_j, rows_c, rows_p, turned):
    core = lax.rem(ids[0], 2)
    for e in range(6):
        near, far = inv_mine[e], inv_other[e]
        first = jnp.where(core == 0, near, far)
        second = jnp.where(core == 0, far, near)
        pieces = []
        for half in (first, second):
            for g in range(4):
                pieces.append(jnp.broadcast_to(half[g : g + 1], (4, 128)))
        table[e] = jnp.concatenate(pieces, axis=0)
    cams = cam[...]
    live = (cams < NCAM).astype(F32)
    tracks = [jnp.concatenate([jac_point[0, v], jac_point[1, v]], axis=0) * live for v in range(6)]
    spots = pt[...]
    eliminate(tracks, spots, table, rows_e)
    rows_c[...] = cams.astype(F32)
    rows_p[...] = spots.astype(F32)
    for v in range(12):
        rows_j[v] = jnp.concatenate([jac_cam[0, v], jac_cam[1, v]], axis=0)

    def block(q, carry):
        here = pl.ds(q, 1)
        hot_c = hot(rows_c[here], NCAM)
        hot_p = hot(rows_p[here], PTS)
        left = {}
        right = {}
        for r in range(2):
            hi_k, lo_k, hi_i, lo_i = [], [], [], []
            for k in range(6):
                hi, lo = split(rows_j[6 * r + k, here])
                hi_k.append(spread(hi, hot_p))
                lo_k.append(spread(lo, hot_p))
            for i in (0, 1, 2, 2):
                hi, lo = split(rows_e[3 * r + i, here])
                hi_i.append(spread(hi, hot_c))
                lo_i.append(spread(lo, hot_c))
            left[r] = (jnp.concatenate(hi_k, axis=0), jnp.concatenate(lo_k, axis=0))
            right[r] = (jnp.concatenate(hi_i, axis=0), jnp.concatenate(lo_i, axis=0))
        lhs = jnp.concatenate([left[0][0], left[1][0], left[0][1], left[1][1], left[0][0], left[1][0]], axis=1)
        rhs = jnp.concatenate([right[0][0], right[1][0], right[0][0], right[1][0], right[0][1], right[1][1]], axis=1)
        tile = lax.dot_general(lhs, rhs, NT, preferred_element_type=F32)

        def store(i, m, value):
            at = pl.multiple_of(q * 96 + 32 * i, 32)
            turned[pl.ds(at, 32), 128 * m : 128 * m + 128] = value.astype(BF16)

        relayout(tile, store)
        return carry

    lax.fori_loop(0, Q, block, 0, unroll=2)
    row = lax.broadcasted_iota(jnp.int32, (ROWS, ROWS), 0)
    col = lax.broadcasted_iota(jnp.int32, (ROWS, ROWS), 1)
    order = jnp.where((row // 6 == lax.rem(col, NCAM)) & (lax.rem(row, 6) == col // NCAM), 1.0, 0.0).astype(BF16)
    panel[...] = lax.dot_general(order, turned[...], NT, preferred_element_type=F32).astype(BF16)


def tiles_kernel(n, first, *refs):
    ids = refs[0]
    payloads = refs[1 : 1 + n]
    table, panel = refs[1 + n : 3 + n]
    rest = refs[3 + n :]
    if not first:
        rest = rest[1:]
    out, rows_e, rows_j, rows_c, rows_p, turned, product, shown, sems = rest
    core = lax.rem(ids[0], 2)
    lane = lax.broadcasted_iota(jnp.int32, (8, 128), 1)
    sources = []
    picks = []
    for m in range(3):
        at = 128 * m + lane
        source = lax.rem(at, 6) * NCAM + at // 6
        sources.append(lax.rem(source, 128))
        picks.append(source // 128)

    def copy(t, j):
        column = ids[1 + t] * (2 * ROWS) + ROWS * lax.rem(core + j, 2)
        target = out.at[:, pl.ds(pl.multiple_of(column, 128), ROWS)]
        return pltpu.make_async_copy(shown.at[t % 2, j], target, sems.at[t % 2, j])

    for t in range(n):
        payload = payloads[t]
        for j in range(2):
            spots = payload[j, 25].astype(F32)
            tracks = [payload[j, 12 + v].astype(F32) + payload[j, 18 + v].astype(F32) for v in range(6)]
            eliminate(tracks, spots.astype(jnp.int32), table, rows_e)
            rows_c[...] = payload[j, 24].astype(F32)
            rows_p[...] = spots
            for v in range(12):
                rows_j[v] = payload[j, v].astype(F32)

            def block(q, carry):
                here = pl.ds(q, 1)
                hot_c = hot(rows_c[here], NCAM)
                hot_p = hot(rows_p[here], PTS)
                left = []
                right = []
                for r in range(2):
                    left.append(jnp.concatenate([spread(rows_j[6 * r + k, here], hot_p) for k in range(6)], axis=0))
                    cols = [spread(rows_e[3 * r + i, here], hot_c) for i in range(3)]
                    right.append(jnp.concatenate(cols + [cols[2]], axis=0))
                tile = lax.dot_general(
                    jnp.concatenate(left, axis=1), jnp.concatenate(right, axis=1), NT, preferred_element_type=F32
                )

                def store(i, m, value):
                    at = pl.multiple_of(q * 96 + 32 * i, 32)
                    turned[pl.ds(at, 32), ROWS * j + 128 * m : ROWS * j + 128 * m + 128] = value.astype(BF16)

                relayout(tile, store)
                return carry

            lax.fori_loop(0, Q, block, 0, unroll=8)
        product[...] = jnp.dot(panel[...], turned[...], preferred_element_type=F32)
        if t >= 2:
            for j in range(2):
                copy(t - 2, j).wait()

        def reorder(g, carry):
            rows = pl.ds(pl.multiple_of(g * 8, 8), 8)
            for j in range(2):
                got = [product[rows, ROWS * j + 128 * s : ROWS * j + 128 * s + 128] for s in range(3)]
                for m in range(3):
                    moved = [jnp.take_along_axis(x, sources[m], axis=1) for x in got]
                    value = jnp.where(picks[m] == 0, moved[0], jnp.where(picks[m] == 1, moved[1], moved[2]))
                    shown[t % 2, j, rows, 128 * m : 128 * m + 128] = value
            return carry

        lax.fori_loop(0, ROWS // 8, reorder, 0, unroll=8)
        for j in range(2):
            copy(t, j).start()
    for t in range(max(0, n - 2), n):
        for j in range(2):
            copy(t, j).wait()


def tiles(ids, payloads, table, panel, out):
    n = len(payloads)
    first = out is None
    specs = [smem()] + [vmem()] * (n + 2)
    args = [ids, *payloads, table, panel]
    aliases = {}
    if not first:
        specs.append(pl.BlockSpec(memory_space=pl.ANY))
        args.append(out)
        aliases = {len(args) - 1: 0}
    return pl.pallas_call(
        functools.partial(tiles_kernel, n, first),
        out_shape=jax.ShapeDtypeStruct((ROWS, NBLK * ROWS), F32),
        in_specs=specs,
        out_specs=pl.BlockSpec(memory_space=pl.ANY),
        input_output_aliases=aliases,
        scratch_shapes=[
            pltpu.VMEM((6, Q, 128), F32),
            pltpu.VMEM((12, Q, 128), F32),
            pltpu.VMEM((Q, 128), F32),
            pltpu.VMEM((Q, 128), F32),
            pltpu.VMEM((DEPTH, 2 * ROWS), BF16),
            pltpu.VMEM((ROWS, 2 * ROWS), F32),
            pltpu.VMEM((2, 2, ROWS, ROWS), F32),
            pltpu.SemaphoreType.DMA((2, 2)),
        ],
        compiler_params=params(),
    )(*args)


def body(cam_index, point_index, jac_cam, jac_point, point_damping):
    cam = cam_index.reshape(Q, 128)
    pt = point_index.reshape(Q, 128)
    jac_cam = jac_cam.reshape(2, 12, NBLK, 128)
    jac_point = jac_point.reshape(2, 6, NBLK, 128)
    damping = point_damping.reshape(1, PTS)
    here = lax.axis_index("blk")
    chip = here // 2
    swap = [(n, n ^ 1) for n in range(NBLK)]

    def ids(*steps):
        return jnp.stack([here] + [lax.rem(chip + 8 - s, 8) for s in steps]).astype(jnp.int32)

    only = ids()
    shape = jax.ShapeDtypeStruct
    payload, mine, other = pl.pallas_call(
        prepare,
        out_shape=(shape((VALS, Q, 128), BF16), shape((4, 8, 128), F32), shape((4, 8, 128), F32)),
        in_specs=[smem()] + [vmem()] * 5,
        out_specs=(vmem(),) * 3,
        scratch_shapes=[pltpu.VMEM((Q, 8, 128), F32)],
        compiler_params=params(),
    )(only, cam, pt, jac_cam, jac_point, damping)
    pair_sum = mine + lax.ppermute(other, "blk", swap)
    local = jnp.stack([payload, lax.ppermute(payload, "blk", swap)])
    ups = [local]
    downs = [local]
    up_pairs = [(n, (n + 2) % NBLK) for n in range(NBLK)]
    down_pairs = [(n, (n - 2) % NBLK) for n in range(NBLK)]
    for step in range(4):
        ups.append(lax.ppermute(ups[-1], "blk", up_pairs))
        if step < 3:
            downs.append(lax.ppermute(downs[-1], "blk", down_pairs))
    groups = []
    for s in range(16):
        after = (s + 1) % 16
        groups.append([s * NBLK + 2 * z + 1 for z in range(8)] + [after * NBLK + 2 * z for z in range(8)])
    parts = lax.all_to_all(
        jnp.broadcast_to(pair_sum[None], (16, 4, 8, 128)),
        ("cam", "blk"),
        split_axis=0,
        concat_axis=0,
        axis_index_groups=groups,
        tiled=True,
    )
    inverse = pl.pallas_call(
        factor,
        out_shape=shape((6, 4, 128), F32),
        in_specs=[vmem()],
        out_specs=vmem(),
        compiler_params=params(),
    )(parts)
    inverse_other = lax.ppermute(inverse, "blk", swap)
    panel, table = pl.pallas_call(
        own_panel,
        out_shape=(shape((ROWS, DEPTH), BF16), shape((6, Q, 128), F32)),
        in_specs=[smem()] + [vmem()] * 6,
        out_specs=(vmem(),) * 2,
        scratch_shapes=[
            pltpu.VMEM((6, Q, 128), F32),
            pltpu.VMEM((12, Q, 128), F32),
            pltpu.VMEM((Q, 128), F32),
            pltpu.VMEM((Q, 128), F32),
            pltpu.VMEM((DEPTH, ROWS), BF16),
        ],
        compiler_params=params(),
    )(only, cam, pt, jac_cam, jac_point, inverse, inverse_other)
    out = tiles(ids(0), [local], table, panel, None)
    out = tiles(ids(1, -1), [ups[1], downs[1]], table, panel, out)
    out = tiles(ids(2, -2), [ups[2], downs[2]], table, panel, out)
    out = tiles(ids(3, -3, 4), [ups[3], downs[3], ups[4]], table, panel, out)
    return out


def solution(mesh):
    return jax.shard_map(
        body,
        mesh=mesh,
        in_specs=(
            P("cam", "blk", None, None, None),
            P("cam", "blk", None, None, None),
            P("cam", "blk", None, None, None, None),
            P("cam", "blk", None, None, None, None),
            P("cam", "blk", None),
        ),
        out_specs=P(("cam", "blk"), None),
        check_vma=False,
    )
```

time: 364 us -> 161 us (0.44)
  waiting for transfers between devices: 221 us -> 27.9 us
  Pallas kernels: 0 us -> 102 us
  local copies, waits for them, and re-layouts: 40.5 us -> 2.81 us
  other arithmetic: 39 us -> 4.28 us
  matrix products: 23.8 us -> 0 us
  between operations: 13.7 us -> 0.42 us
    all_gather x1 -> x0, waiting for transfers between devices: 193 us -> none  [body(): return outer(panel, lax.all_gather(panel, 'blk', axis=0, tiled=True))]
    pallas_call x0 -> x7, Pallas kernels: none -> 102 us  [the longest x4 86.5 us: tiles(): pl.pallas_call(functools.partial(tiles_kernel, n, first), out_shape=jax.S...]
    scatter-add x1 -> x0, other arithmetic: 35.5 us -> none  [build_panel(): summed = jax.ops.segment_sum(values.T, bins, num_segments=NCAM * width)]
    dot_general x2 -> x0, matrix products: 23.8 us -> none  [the longest x1 22.8 us: outer(): lax.dot_general(left, right, (((1,), (1,)), ((), ())), preferred_element_...]
    scatter-add x1 -> x0, local copies, waits for them, and re-layouts: 18.8 us -> none  [build_panel(): summed = jax.ops.segment_sum(values.T, bins, num_segments=NCAM * width)]
    ppermute x3 -> x10, waiting for transfers between devices: 3.98 us -> 21.6 us  [the longest x4 18.8 us: body(): ups.append(lax.ppermute(ups[-1], 'blk', up_pairs))]
    all_to_all x3 -> x1, waiting for transfers between devices: 23.3 us -> 6.29 us  [body(): lax.all_to_all(jnp.broadcast_to(pair_sum[None], (16, 4, 8, 128)), ('cam',...]
    gather x2 -> x0, local copies, waits for them, and re-layouts: 11.4 us -> none  [body(): jnp.take(lookup_table, received_spots[0], axis=1)]
  transfers between devices with their start and end apart: 7 -> 11, of which waited for: 5 -> 6; matrix products, arithmetic and copies ran while one was open for 1% -> 3% of each run, Pallas kernels for 0% -> 43%
where the time goes in v1:
time: 161 us
  Pallas kernels  102 us (63%)
  waiting for transfers between devices  27.9 us (17%)
  starting transfers between devices  23 us (14%)
  other arithmetic  4.28 us (3%)
  local copies, waits for them, and re-layouts  2.81 us (2%)
    pallas_call x4, Pallas kernels, tiles(): pl.pallas_call(functools.partial(tiles_kernel, n, first), out_shape=jax.S...  86.5 us
    ppermute x4, waiting for transfers between devices, body(): ups.append(lax.ppermute(ups[-1], 'blk', up_pairs))  18.8 us
    pallas_call x1, Pallas kernels, body(): pl.pallas_call(own_panel, out_shape=(shape((ROWS, DEPTH), BF16), shape((6...  12.1 us
    ppermute x3, starting transfers between devices, body(): downs.append(lax.ppermute(downs[-1], 'blk', down_pairs))  9.15 us
    all_to_all x1, starting transfers between devices, body(): lax.all_to_all(jnp.broadcast_to(pair_sum[None], (16, 4, 8, 128)), ('cam',...  6.79 us
    all_to_all x1, waiting for transfers between devices, body(): lax.all_to_all(jnp.broadcast_to(pair_sum[None], (16, 4, 8, 128)), ('cam',...  6.29 us
    ppermute x1, starting transfers between devices, body(): local = jnp.stack([payload, lax.ppermute(payload, 'blk', swap)])  3.24 us
  transfers between devices with their start and end apart: 11, of which 6 were waited for; matrix products, arithmetic and copies ran while one was open for 3% of the time, Pallas kernels for 43%

profile of v1, /device:TPU:1, one launch (start us, length us, event | category | flops | bytes accessed | tf_op | source)
XLA Modules:
  0.0 160.8 jit_solution(7243590515578866727)
XLA Ops:
  0.0 2.1 %shard_map.55 = (bf16[26,32,128]{2,1,0:T(8,128)(2,1)}, f32[4,8,128]{2,1,0:T(8,128)}, f32[4,8,128]{2,1,0:T(8,128)}) custom-call(s32[1]{0:T(128)} %bitcast.ids, s32[32,128]{1,0:T(8,128)} %bitcast.22, s32[32,128]{1,0:T(8,128)} %bitcast.24, f32[2,12,16,128]{3,2,1,0:T(8,128)} %bitcast.16, f32[2,6,16,128]{3,2,1,0:T(8,128)} %bitcast.18, f32[1,32]{1,0:T(1,128)} %bitcast.26), custom_call_target="tpu_custom_call" | custom-call | tf_op jit(solution)/shard_map/pallas_call | solution.py:323
  2.1 3.2 %collective-permute-start = (bf16[26,32,128]{2,1,0:T(8,128)(2,1)}, bf16[26,32,128]{2,1,0:T(8,128)(2,1)S(1)}, u32[]{:S(2)}, u32[]{:S(2)}) collective-permute-start(bf16[26,32,128]{2,1,0:T(8,128)(2,1)} %get-tuple-element.10), channel_id=1, source_target_pairs={{0,1},{1,0},{2,3},{3,2},{4,5},{5,4},{6,7},{7,6},{8,9},{9,8},{10,11... | collective-permute-start | bytes 638984 | tf_op jit(solution)/shard_map/ppermute | solution.py:332
  5.4 1.3 collective-permute-done
  6.7 1.0 pad_maximum_fusion.refs_1_
  7.7 3.9 %collective-permute-start.4 = (bf16[2,26,32,128]{3,2,1,0:T(8,128)(2,1)S(1)}, bf16[2,26,32,128]{3,2,1,0:T(8,128)(2,1)S(1)}, u32[]{:S(2)}, u32[]{:S(2)}) collective-permute-start(bf16[2,26,32,128]{3,2,1,0:T(8,128)(2,1)S(1)} %pad_maximum_fusion.refs_1_), channel_id=1, source_target_pairs={{0,14},{1,15},{2,0},{3,1},{4,2},{5,3},{6,4},{7,5},{8,6},{9,7},{10,... | collective-permute-start | bytes 1277960 | tf_op jit(solution)/shard_map/ppermute | solution.py:340
  11.7 9.8 %collective-permute-done.1.refs_1_ = bf16[2,26,32,128]{3,2,1,0:T(8,128)(2,1)S(1)} collective-permute-done((bf16[2,26,32,128]{3,2,1,0:T(8,128)(2,1)S(1)}, bf16[2,26,32,128]{3,2,1,0:T(8,128)(2,1)S(1)}, u32[]{:S(2)}, u32[]{:S(2)}) %collective-permute-start.1) | collective-permute-done | bytes 426016 | tf_op jit(solution)/shard_map/ppermute | solution.py:338
  21.5 2.7 %collective-permute-start.5 = (bf16[2,26,32,128]{3,2,1,0:T(8,128)(2,1)S(1)}, bf16[2,26,32,128]{3,2,1,0:T(8,128)(2,1)S(1)}, u32[]{:S(2)}, u32[]{:S(2)}) collective-permute-start(bf16[2,26,32,128]{3,2,1,0:T(8,128)(2,1)S(1)} %collective-permute-done.4.refs_2_), channel_id=1, source_target_pairs={{0,14},{1,15},{2,0},{3,1},{4,2},{5,3},{6,4},{7,5},{8,6},{9,7},{10,... | collective-permute-start | bytes 1277960 | tf_op jit(solution)/shard_map/ppermute | solution.py:340
  24.1 9.0 %collective-permute-done.2.refs_1_ = bf16[2,26,32,128]{3,2,1,0:T(8,128)(2,1)S(1)} collective-permute-done((bf16[2,26,32,128]{3,2,1,0:T(8,128)(2,1)S(1)}, bf16[2,26,32,128]{3,2,1,0:T(8,128)(2,1)S(1)}, u32[]{:S(2)}, u32[]{:S(2)}) %collective-permute-start.2) | collective-permute-done | bytes 426016 | tf_op jit(solution)/shard_map/ppermute | solution.py:338
  33.1 1.8 %collective-permute-start.8 = (f32[4,8,128]{2,1,0:T(8,128)}, f32[4,8,128]{2,1,0:T(8,128)S(1)}, u32[]{:S(2)}, u32[]{:S(2)}) collective-permute-start(f32[4,8,128]{2,1,0:T(8,128)} %get-tuple-element.12), channel_id=1, source_target_pairs={{0,1},{1,0},{2,3},{3,2},{4,5},{5,4},{6,7},{7,6},{8,9},{9,8},{10,11... | collective-permute-start | bytes 49160 | tf_op jit(solution)/shard_map/ppermute | solution.py:331
  34.9 1.0 collective-permute-done.8
  36.0 0.7 add.35
  36.7 0.7 broadcast_in_dim.2
  37.4 6.8 %all-to-all-start = ((f32[16,4,8,128]{3,2,1,0:T(8,128)}), f32[16,4,8,128]{3,2,1,0:T(8,128)S(1)}, u32[]{:S(2)}, u32[]{:S(2)}) async-start(f32[16,4,8,128]{3,2,1,0:T(8,128)} %broadcast_in_dim.2), calls=%async_computation | async-start | bytes 524288 | tf_op jit(solution)/shard_map/all_to_all | solution.py:345
  44.3 2.6 %collective-permute-start.6 = (bf16[2,26,32,128]{3,2,1,0:T(8,128)(2,1)S(1)}, bf16[2,26,32,128]{3,2,1,0:T(8,128)(2,1)S(1)}, u32[]{:S(2)}, u32[]{:S(2)}) collective-permute-start(bf16[2,26,32,128]{3,2,1,0:T(8,128)(2,1)S(1)} %collective-permute-done.5.refs_2_), channel_id=1, source_target_pairs={{0,14},{1,15},{2,0},{3,1},{4,2},{5,3},{6,4},{7,5},{8,6},{9,7},{10,... | collective-permute-start | bytes 1277960 | tf_op jit(solution)/shard_map/ppermute | solution.py:340
  46.9 0.7 pad_add_fusion.3.refs_0_
  48.9 6.3 %all-to-all-done.parts = f32[16,4,8,128]{3,2,1,0:T(8,128)S(1)} async-done(((f32[16,4,8,128]{3,2,1,0:T(8,128)}), f32[16,4,8,128]{3,2,1,0:T(8,128)S(1)}, u32[]{:S(2)}, u32[]{:S(2)}) %all-to-all-start) | async-done | bytes 262176 | tf_op jit(solution)/shard_map/all_to_all | solution.py:345
  55.8 1.6 %shard_map.56.inv_mine = f32[6,4,128]{2,1,0:T(4,128)} custom-call(f32[16,4,8,128]{3,2,1,0:T(8,128)} %copy-done.1), custom_call_target="tpu_custom_call" | custom-call | tf_op jit(solution)/shard_map/pallas_call | solution.py:353
  57.5 2.0 %collective-permute-start.9 = (f32[6,4,128]{2,1,0:T(4,128)}, f32[6,4,128]{2,1,0:T(4,128)S(1)}, u32[]{:S(2)}, u32[]{:S(2)}) collective-permute-start(f32[6,4,128]{2,1,0:T(4,128)} %shard_map.56.inv_mine), channel_id=1, source_target_pairs={{0,1},{1,0},{2,3},{3,2},{4,5},{5,4},{6,7},{7,6},{8,9},{9,8},{10,11... | collective-permute-start | bytes 36872 | tf_op jit(solution)/shard_map/ppermute | solution.py:360
  61.1 12.1 %shard_map.57 = (bf16[384,3072]{1,0:T(8,128)(2,1)}, f32[6,32,128]{2,1,0:T(8,128)}) custom-call(s32[1]{0:T(128)} %bitcast.ids, s32[32,128]{1,0:T(8,128)} %bitcast.23, s32[32,128]{1,0:T(8,128)} %bitcast.25, f32[2,12,16,128]{3,2,1,0:T(8,128)} %bitcast.17, f32[2,6,16,128]{3,2,1,0:T(8,128)} %bitcast.19, f32[6,4,128]{2,1,0:T(4,128)} %shard_map.56.inv_mine, ...), custom_call_target="tpu_custom_call" | custom-call | tf_op jit(solution)/shard_map/pallas_call | solution.py:361
  73.2 12.2 %shard_map.58.refs_5_ = f32[384,6144]{1,0:T(8,128)} custom-call(s32[2]{0:T(128)} %pad_add_fusion.3.refs_0_, bf16[2,26,32,128]{3,2,1,0:T(8,128)(2,1)} %copy-done, f32[6,32,128]{2,1,0:T(8,128)} %get-tuple-element.13.refs_2_.refs_3_.refs_4_, bf16[384,3072]{1,0:T(8,128)(2,1)} %get-tuple-element.14.refs_3_.refs_4_.refs_5_), custom_call_target="tpu_custom_call" | custom-call | tf_op jit(solution)/shard_map/pallas_call | solution.py:288
  85.4 21.6 %shard_map.59.refs_5_ = f32[384,6144]{1,0:T(8,128)} custom-call(s32[3]{0:T(128)} %pad_add_fusion.2.refs_0_, bf16[2,26,32,128]{3,2,1,0:T(8,128)(2,1)} %copy-done.2, bf16[2,26,32,128]{3,2,1,0:T(8,128)(2,1)} %copy-done.3, f32[6,32,128]{2,1,0:T(8,128)} %get-tuple-element.13.refs_2_.refs_3_.refs_4_, ...), custom_call_target="tpu_custom_call", output_to_operand_aliasing={{}: (5, {})} | custom-call | tf_op jit(solution)/shard_map/pallas_call | solution.py:288
  107.0 21.8 %shard_map.60.refs_6_ = f32[384,6144]{1,0:T(8,128)} custom-call(s32[3]{0:T(128)} %pad_add_fusion.1.refs_0_, bf16[2,26,32,128]{3,2,1,0:T(8,128)(2,1)} %copy-done.4, bf16[2,26,32,128]{3,2,1,0:T(8,128)(2,1)} %copy-done.6, f32[6,32,128]{2,1,0:T(8,128)} %get-tuple-element.13.refs_2_.refs_3_.refs_4_, ...), custom_call_target="tpu_custom_call", output_to_operand_aliasing={{}: (5, {})} | custom-call | tf_op jit(solution)/shard_map/pallas_call | solution.py:288
  128.8 0.8 copy-done.7
  129.6 31.0 %shard_map.61 = f32[384,6144]{1,0:T(8,128)} custom-call(s32[4]{0:T(128)} %pad_add_fusion.refs_0_, bf16[2,26,32,128]{3,2,1,0:T(8,128)(2,1)} %copy-done.5, bf16[2,26,32,128]{3,2,1,0:T(8,128)(2,1)} %copy-done.7, bf16[2,26,32,128]{3,2,1,0:T(8,128)(2,1)} %collective-permute-done.7.refs_3_, ...), custom_call_target="tpu_custom_call", output_to_operand_aliasing={{}: (6, {})} | custom-call | tf_op jit(solution)/shard_map/pallas_call | solution.py:288
  (30 shorter events, 3.7 us)
Async XLA Ops:
  2.1 4.5 %collective-permute-start = (bf16[26,32,128]{2,1,0:T(8,128)(2,1)}, bf16[26,32,128]{2,1,0:T(8,128)(2,1)S(1)}, u32[]{:S(2)}, u32[]{:S(2)}) collective-permute-start(bf16[26,32,128]{2,1,0:T(8,128)(2,1)} %get-tuple-element.10), channel_id=1, source_target_pairs={{0,1},{1,0},{2,3},{3,2},{4,5},{5,4},{6,7},{7,6},{8,9},{9,8},{10,11... | collective-permute-start | bytes 638984 | tf_op jit(solution)/shard_map/ppermute | solution.py:332
  7.6 65.6 %copy-start = (bf16[2,26,32,128]{3,2,1,0:T(8,128)(2,1)}, bf16[2,26,32,128]{3,2,1,0:T(8,128)(2,1)S(1)}, u32[]{:S(2)}) copy-start(bf16[2,26,32,128]{3,2,1,0:T(8,128)(2,1)S(1)} %pad_maximum_fusion.refs_1_) | copy-start | bytes 1277956
  7.6 13.8 %collective-permute-start.1 = (bf16[2,26,32,128]{3,2,1,0:T(8,128)(2,1)S(1)}, bf16[2,26,32,128]{3,2,1,0:T(8,128)(2,1)S(1)}, u32[]{:S(2)}, u32[]{:S(2)}) collective-permute-start(bf16[2,26,32,128]{3,2,1,0:T(8,128)(2,1)S(1)} %pad_maximum_fusion.refs_1_), channel_id=1, source_target_pairs={{0,2},{1,3},{2,4},{3,5},{4,6},{5,7},{6,8},{7,9},{8,10},{9,11},{10,... | collective-permute-start | bytes 1277960 | tf_op jit(solution)/shard_map/ppermute | solution.py:338
  7.7 13.7 %collective-permute-start.4 = (bf16[2,26,32,128]{3,2,1,0:T(8,128)(2,1)S(1)}, bf16[2,26,32,128]{3,2,1,0:T(8,128)(2,1)S(1)}, u32[]{:S(2)}, u32[]{:S(2)}) collective-permute-start(bf16[2,26,32,128]{3,2,1,0:T(8,128)(2,1)S(1)} %pad_maximum_fusion.refs_1_), channel_id=1, source_target_pairs={{0,14},{1,15},{2,0},{3,1},{4,2},{5,3},{6,4},{7,5},{8,6},{9,7},{10,... | collective-permute-start | bytes 1277960 | tf_op jit(solution)/shard_map/ppermute | solution.py:340
  21.5 64.0 %copy-start.2 = (bf16[2,26,32,128]{3,2,1,0:T(8,128)(2,1)}, bf16[2,26,32,128]{3,2,1,0:T(8,128)(2,1)S(1)}, u32[]{:S(2)}) copy-start(bf16[2,26,32,128]{3,2,1,0:T(8,128)(2,1)S(1)} %collective-permute-done.1.refs_1_) | copy-start | bytes 1277956
  21.5 11.7 %collective-permute-start.2 = (bf16[2,26,32,128]{3,2,1,0:T(8,128)(2,1)S(1)}, bf16[2,26,32,128]{3,2,1,0:T(8,128)(2,1)S(1)}, u32[]{:S(2)}, u32[]{:S(2)}) collective-permute-start(bf16[2,26,32,128]{3,2,1,0:T(8,128)(2,1)S(1)} %collective-permute-done.1.refs_1_), channel_id=1, source_target_pairs={{0,2},{1,3},{2,4},{3,5},{4,6},{5,7},{6,8},{7,9},{8,10},{9,11},{10,... | collective-permute-start | bytes 1277960 | tf_op jit(solution)/shard_map/ppermute | solution.py:338
  21.5 64.0 %copy-start.3 = (bf16[2,26,32,128]{3,2,1,0:T(8,128)(2,1)}, bf16[2,26,32,128]{3,2,1,0:T(8,128)(2,1)S(1)}, u32[]{:S(2)}) copy-start(bf16[2,26,32,128]{3,2,1,0:T(8,128)(2,1)S(1)} %collective-permute-done.4.refs_2_) | copy-start | bytes 1277956
  21.5 22.8 %collective-permute-start.5 = (bf16[2,26,32,128]{3,2,1,0:T(8,128)(2,1)S(1)}, bf16[2,26,32,128]{3,2,1,0:T(8,128)(2,1)S(1)}, u32[]{:S(2)}, u32[]{:S(2)}) collective-permute-start(bf16[2,26,32,128]{3,2,1,0:T(8,128)(2,1)S(1)} %collective-permute-done.4.refs_2_), channel_id=1, source_target_pairs={{0,14},{1,15},{2,0},{3,1},{4,2},{5,3},{6,4},{7,5},{8,6},{9,7},{10,... | collective-permute-start | bytes 1277960 | tf_op jit(solution)/shard_map/ppermute | solution.py:340
  33.1 73.9 %copy-start.4 = (bf16[2,26,32,128]{3,2,1,0:T(8,128)(2,1)}, bf16[2,26,32,128]{3,2,1,0:T(8,128)(2,1)S(1)}, u32[]{:S(2)}) copy-start(bf16[2,26,32,128]{3,2,1,0:T(8,128)(2,1)S(1)} %collective-permute-done.2.refs_1_) | copy-start | bytes 1277956
  33.1 13.8 %collective-permute-start.3 = (bf16[2,26,32,128]{3,2,1,0:T(8,128)(2,1)S(1)}, bf16[2,26,32,128]{3,2,1,0:T(8,128)(2,1)S(1)}, u32[]{:S(2)}, u32[]{:S(2)}) collective-permute-start(bf16[2,26,32,128]{3,2,1,0:T(8,128)(2,1)S(1)} %collective-permute-done.2.refs_1_), channel_id=1, source_target_pairs={{0,2},{1,3},{2,4},{3,5},{4,6},{5,7},{6,8},{7,9},{8,10},{9,11},{10,... | collective-permute-start | bytes 1277960 | tf_op jit(solution)/shard_map/ppermute | solution.py:338
  33.1 2.8 %collective-permute-start.8 = (f32[4,8,128]{2,1,0:T(8,128)}, f32[4,8,128]{2,1,0:T(8,128)S(1)}, u32[]{:S(2)}, u32[]{:S(2)}) collective-permute-start(f32[4,8,128]{2,1,0:T(8,128)} %get-tuple-element.12), channel_id=1, source_target_pairs={{0,1},{1,0},{2,3},{3,2},{4,5},{5,4},{6,7},{7,6},{8,9},{9,8},{10,11... | collective-permute-start | bytes 49160 | tf_op jit(solution)/shard_map/ppermute | solution.py:331
  37.4 17.7 %all-to-all-start = ((f32[16,4,8,128]{3,2,1,0:T(8,128)}), f32[16,4,8,128]{3,2,1,0:T(8,128)S(1)}, u32[]{:S(2)}, u32[]{:S(2)}) async-start(f32[16,4,8,128]{3,2,1,0:T(8,128)} %broadcast_in_dim.2), calls=%async_computation | async-start | bytes 524288 | tf_op jit(solution)/shard_map/all_to_all | solution.py:345
  44.3 62.7 %copy-start.6 = (bf16[2,26,32,128]{3,2,1,0:T(8,128)(2,1)}, bf16[2,26,32,128]{3,2,1,0:T(8,128)(2,1)S(1)}, u32[]{:S(2)}) copy-start(bf16[2,26,32,128]{3,2,1,0:T(8,128)(2,1)S(1)} %collective-permute-done.5.refs_2_) | copy-start | bytes 1277956
  44.3 84.5 %collective-permute-start.6 = (bf16[2,26,32,128]{3,2,1,0:T(8,128)(2,1)S(1)}, bf16[2,26,32,128]{3,2,1,0:T(8,128)(2,1)S(1)}, u32[]{:S(2)}, u32[]{:S(2)}) collective-permute-start(bf16[2,26,32,128]{3,2,1,0:T(8,128)(2,1)S(1)} %collective-permute-done.5.refs_2_), channel_id=1, source_target_pairs={{0,14},{1,15},{2,0},{3,1},{4,2},{5,3},{6,4},{7,5},{8,6},{9,7},{10,... | collective-permute-start | bytes 1277960 | tf_op jit(solution)/shard_map/ppermute | solution.py:340
  46.9 81.9 %copy-start.5 = (bf16[2,26,32,128]{3,2,1,0:T(8,128)(2,1)}, bf16[2,26,32,128]{3,2,1,0:T(8,128)(2,1)S(1)}, u32[]{:S(2)}) copy-start(bf16[2,26,32,128]{3,2,1,0:T(8,128)(2,1)S(1)} %collective-permute-done.3.refs_1_) | copy-start | bytes 1277956
  46.9 82.0 %collective-permute-start.7 = (bf16[2,26,32,128]{3,2,1,0:T(8,128)(2,1)S(1)}, bf16[2,26,32,128]{3,2,1,0:T(8,128)(2,1)}, u32[]{:S(2)}, u32[]{:S(2)}) collective-permute-start(bf16[2,26,32,128]{3,2,1,0:T(8,128)(2,1)S(1)} %collective-permute-done.3.refs_1_), channel_id=1, source_target_pairs={{0,2},{1,3},{2,4},{3,5},{4,6},{5,7},{6,8},{7,9},{8,10},{9,11},{10,... | collective-permute-start | bytes 1277960 | tf_op jit(solution)/shard_map/ppermute | solution.py:338
  55.1 0.7 copy-start.1
  57.5 3.0 %collective-permute-start.9 = (f32[6,4,128]{2,1,0:T(4,128)}, f32[6,4,128]{2,1,0:T(4,128)S(1)}, u32[]{:S(2)}, u32[]{:S(2)}) collective-permute-start(f32[6,4,128]{2,1,0:T(4,128)} %shard_map.56.inv_mine), channel_id=1, source_target_pairs={{0,1},{1,0},{2,3},{3,2},{4,5},{5,4},{6,7},{7,6},{8,9},{9,8},{10,11... | collective-permute-start | bytes 36872 | tf_op jit(solution)/shard_map/ppermute | solution.py:360
  60.5 0.6 copy-start.8
  128.8 0.8 copy-start.7
